TPU v7x, 128 devices: a whole 4x4x4 slice. The times are simulated.
128 devices in a mesh: wide: 16 (over z, x), narrow: 8 (over y, core).
Axes of the slice: x: 4, y: 4, z: 4, core: 2. Of those that a mesh axis runs over, the one named last changes fastest.
Arguments:
- cotangent: float32 [1536, 256, 256], P(('wide', 'narrow')), may hold values from -6 to 6
- row_basis: float32 [1536, 256, 128], P(('wide', 'narrow')), may hold values from -0.375 to 0.375
- col_basis: float32 [1536, 256, 128], P(('wide', 'narrow')), may hold values from -0.5 to 0.5
- leaf_up: float32 [1536, 128, 128], P(('wide', 'narrow')), may hold values from -0.15625 to 0.15625
- node_up: float32 [128, 128, 128], P(('wide', 'narrow')), may hold values from -0.1875 to 0.1875
- node_couple: float32 [128, 2, 128, 128], P(('wide', 'narrow')), may hold values from -0.375 to 0.375
- group_couple: float32 [16, 8, 128, 128], P('wide', 'narrow'), may hold values from -0.1875 to 0.1875
- node_down: float32 [128, 128, 128], P(('wide', 'narrow')), may hold values from -0.5 to 0.5
- leaf_down: float32 [1536, 128, 128], P(('wide', 'narrow')), may hold values from -0.5 to 0.5
- near_blocks: float32 [1536, 4, 256, 256], P(('wide', 'narrow')), may hold values from -0.1875 to 0.1875
- near_index: int32 [1536, 4], P(('wide', 'narrow')), may hold values from 0 to 1535, as said below
- far_nodes: int32 [128, 2], P(('wide', 'narrow')), may hold values from 0 to 7, as said below
- far_groups: int32 [16, 8], P('wide', 'narrow'), may hold values from 0 to 15, as said below
Outputs:
- product: float32 [1536, 256, 256], P(('wide', 'narrow'))
Inputs may be any that keep to these rules, and one draw needn't show every extreme that they name: near_index[l, 0] is l; every other entry differs from l by 1 to 2. far_nodes[d, j] never equals d % 8; the entries of a row differ. far_groups[g, j] never equals g; the entries of a row differ.
All inputs are finite; a program needn't handle non-finite values.
Results may differ from a plain program's by a relative error of at most 0.000062.
Values sent between devices are 32-bit elements; how exact they have to be, the bound alone decides.
A program may use at most 128 MiB of HBM per device.

v0:
```python
import jax
import jax.numpy as jnp
from jax import lax
from jax.sharding import PartitionSpec as P

NEAR_REACH = 2


HIGH = lax.Precision.HIGHEST


def from_behind(value, axis, steps):
    count = lax.axis_size(axis)
    leading, last = (max(0, -steps), min(count, count - steps))
    return lax.ppermute(value, axis, [(source, source + steps) for source in range(leading, last)])


def shards(
    cotangent,
    row_basis,
    col_basis,
    leaf_up,
    node_up,
    node_couple,
    group_couple,
    node_down,
    leaf_down,
    near_blocks,
    near_index,
    far_nodes,
    far_groups,
):
    leaves = cotangent.shape[0]
    lower = from_behind(cotangent[leaves - NEAR_REACH :], ("wide", "narrow"), 1)
    upper = from_behind(cotangent[:NEAR_REACH], ("wide", "narrow"), -1)
    leaf_coeffs = jnp.einsum("lpk,lpv->lkv", row_basis, cotangent, precision=HIGH)
    node_coeffs = jnp.einsum("lkm,lkv->mv", leaf_up, leaf_coeffs, precision=HIGH)
    up_term = jnp.dot(node_up[0].T, node_coeffs, precision=HIGH)
    siblings = lax.all_gather(node_coeffs[None], "narrow", axis=0, tiled=True)
    group_coeffs = lax.psum(up_term, "narrow")
    picked = siblings[far_nodes[0]]
    node_out = jnp.einsum("jkm,jkv->mv", node_couple[0], picked, precision=HIGH)
    all_groups = lax.all_gather(group_coeffs[None], "wide", axis=0, tiled=True)
    picked_groups = all_groups[far_groups[0]]
    partial_value = jnp.einsum("jkm,jkv->mv", group_couple[0], picked_groups, precision=HIGH)
    group_out = lax.psum(partial_value, "narrow")
    node_total = node_out + jnp.dot(node_down[0], group_out, precision=HIGH)
    leaf_total = jnp.einsum("lmk,kv->lmv", leaf_down, node_total, precision=HIGH)
    far_part = jnp.einsum("lpk,lkv->lpv", col_basis, leaf_total, precision=HIGH)
    extended = jnp.concatenate([lower, cotangent, upper], axis=0)
    node_rank = lax.axis_index("wide") * lax.axis_size("narrow") + lax.axis_index("narrow")
    first_leaf = node_rank * leaves - NEAR_REACH
    local_index = near_index - first_leaf
    sources = extended[local_index]
    near_part = jnp.einsum("ljpq,ljpv->lqv", near_blocks, sources, precision=HIGH)
    return far_part + near_part


def solution(mesh):
    in_specs = (
        P(("wide", "narrow"), None, None),
        P(("wide", "narrow"), None, None),
        P(("wide", "narrow"), None, None),
        P(("wide", "narrow"), None, None),
        P(("wide", "narrow"), None, None),
        P(("wide", "narrow"), None, None, None),
        P("wide", "narrow", None, None),
        P(("wide", "narrow"), None, None),
        P(("wide", "narrow"), None, None),
        P(("wide", "narrow"), None, None, None),
        P(("wide", "narrow"), None),
        P(("wide", "narrow"), None),
        P("wide", "narrow"),
    )
    out_specs = P(("wide", "narrow"), None, None)
    return jax.shard_map(shards, mesh=mesh, in_specs=in_specs, out_specs=out_specs, check_vma=False)
```

profile of v0, /device:TPU:1, one launch (start us, length us, event | category | flops | bytes accessed | tf_op | source)
XLA Modules:
  0.0 258.5 jit_solution(13110974289088481287)
XLA Ops:
  6.5 7.7 %fusion.14 = f32[12,128,256]{1,2,0:T(8,128)S(1)} fusion(f32[12,256,128]{2,1,0:T(8,128)} %param.14, f32[12,256,256]{2,1,0:T(8,128)} %param.13), kind=kOutput, calls=%fused_computation.26 | convolution fusion | flops 1207959552 | bytes 6291456 | tf_op jit(solution)/shard_map/lpk,lpv->lkv/dot_general | solution.py:36
  14.3 1.4 fusion.15
  15.7 0.9 convolution_bitcast_fusion.2
  16.6 0.0 all-reduce.3.cloned.1.call-update
  16.7 0.0 all-gather.6.cloned.1.call-start
  16.7 0.7 all-gather.6.cloned.1.call-update
  17.4 0.0 all-gather.4.cloned.1.call-start
  17.5 59.7 %all-reduce.3.cloned.1.call-done = f32[1,128,256]{1,2,0:T(8,128)} async-done(((f32[1,128,256]{1,2,0:T(8,128)}), f32[1,128,256]{1,2,0:T(8,128)}) %all-reduce.3.cloned.1.call-update) | async-done | bytes 131088 | tf_op jit(solution)/shard_map/psum | solution.py:40
  77.2 1.7 copy.25
  78.8 0.0 all-gather.4.cloned.1.call-update
  78.8 0.0 all-reduce.5.cloned.1.call-start
  78.9 2.1 fusion.13
  81.0 3.6 %collective-permute-start = (f32[2,256,256]{2,1,0:T(8,128)}, f32[2,256,256]{2,1,0:T(8,128)S(1)}, u32[]{:S(2)}, u32[]{:S(2)}) collective-permute-start(f32[2,256,256]{2,1,0:T(8,128)} %get-tuple-element.16), channel_id=1, source_target_pairs={{0,1},{1,2},{2,3},{3,4},{4,5},{5,6},{6,7},{7,8},{8,9},{9,10},{10,1... | collective-permute-start | bytes 1572872 | tf_op jit(solution)/shard_map/ppermute | solution.py:15
  84.6 2.6 collective-permute-start.1
  87.8 0.1 copy.26
  87.9 0.1 reshape.69
  88.1 4.0 %collective-permute-done = f32[2,256,256]{2,1,0:T(8,128)S(1)} collective-permute-done((f32[2,256,256]{2,1,0:T(8,128)}, f32[2,256,256]{2,1,0:T(8,128)S(1)}, u32[]{:S(2)}, u32[]{:S(2)}) %collective-permute-start) | collective-permute-done | bytes 524320 | tf_op jit(solution)/shard_map/ppermute | solution.py:15
  92.1 4.8 %collective-permute-done.1 = f32[2,256,256]{2,1,0:T(8,128)S(1)} collective-permute-done((f32[2,256,256]{2,1,0:T(8,128)S(1)}, f32[2,256,256]{2,1,0:T(8,128)S(1)}, u32[]{:S(2)}, u32[]{:S(2)}) %collective-permute-start.1) | collective-permute-done | bytes 524320 | tf_op jit(solution)/shard_map/ppermute | solution.py:15
  96.9 4.2 %pad_maximum_fusion = f32[16,256,256]{2,1,0:T(8,128)} fusion(f32[2,256,256]{2,1,0:T(8,128)S(1)} %collective-permute-done.1, f32[12,256,256]{2,1,0:T(8,128)} %param.13, f32[2,256,256]{2,1,0:T(8,128)S(1)} %collective-permute-done), kind=kLoop, calls=%fused_computation.2 | loop fusion | flops 2097152 | bytes 8388608 | tf_op jit(solution)/shard_map/concatenate | solution.py:50
  101.1 10.0 %gather_fusion.1 = f32[48,256,256]{2,1,0:T(8,128)} fusion(f32[16,256,256]{2,1,0:T(8,128)} %pad_maximum_fusion, s32[1024]{0:T(1024)S(1)} %pad_clamp_fusion), kind=kCustom, calls=%fused_computation.1 | custom fusion | bytes 25166016 | tf_op jit(solution)/shard_map/gather | solution.py:54
  111.0 1.6 copy.34
  112.6 0.6 gather_fusion
  113.2 41.7 %all-gather.4.cloned.1.call-done = f32[16,128,256]{2,1,0:T(8,128)} async-done(((f32[1,128,256]{2,1,0:T(8,128)}), f32[16,128,256]{2,1,0:T(8,128)}) %all-gather.4.cloned.1.call-update) | async-done | bytes 2097168 | tf_op jit(solution)/shard_map/all_gather | solution.py:43
  154.9 1.9 convolution_bitcast_fusion.1
  156.9 0.0 all-reduce.5.cloned.1.call-update
  156.9 0.6 convolution_bitcast_fusion
  157.5 57.3 %all-reduce.5.cloned.1.call-done = f32[128,256]{0,1:T(8,128)} async-done(((f32[128,256]{0,1:T(8,128)}), f32[128,256]{0,1:T(8,128)}) %all-reduce.5.cloned.1.call-update) | async-done | bytes 131088 | tf_op jit(solution)/shard_map/psum | solution.py:46
  214.8 1.2 fusion.3
  216.0 2.5 fusion.16
  218.5 2.9 %fusion.1 = f32[12,256,256]{2,1,0:T(8,128)S(1)} fusion(f32[12,256,128]{2,1,0:T(8,128)S(1)} %copy-done, f32[256,12,128]{2,0,1:T(8,128)S(1)} %fusion.16), kind=kOutput, calls=%fused_computation.5 | convolution fusion | flops 1207959552 | bytes 6291456 | tf_op jit(solution)/shard_map/lpk,lkv->lpv/dot_general | solution.py:49
  221.4 27.0 %fusion = f32[12,256,256]{1,2,0:T(8,128)} fusion(f32[12,256,256]{2,1,0:T(8,128)S(1)} %fusion.1, f32[12,4,256,256]{3,2,1,0:T(8,128)} %bitcast.62, f32[12,4,256,256]{3,2,1,0:T(8,128)} %param.22), kind=kOutput, calls=%fused_computation.4 | convolution fusion | flops 9664462848 | bytes 31457280 | tf_op jit(solution)/shard_map/ljpq,ljpv->lqv/dot_general | solution.py:55
  248.4 3.5 %copy.28 = f32[12,256,256]{2,1,0:T(8,128)} copy(f32[12,256,256]{1,2,0:T(8,128)} %fusion) | data formatting | bytes 6291456 | tf_op jit(solution)/shard_map/add | solution.py:56
  (24 shorter events, 0.1 us)
Async XLA Ops:
  6.5 212.0 %copy-start = (f32[12,256,128]{2,1,0:T(8,128)S(1)}, f32[12,256,128]{2,1,0:T(8,128)}, u32[]{:S(2)}) copy-start(f32[12,256,128]{2,1,0:T(8,128)} %param.15) | copy-start | bytes 4718596
  6.5 7.7 %copy-start.2 = (f32[12,128,128]{2,1,0:T(8,128)S(1)}, f32[12,128,128]{2,1,0:T(8,128)}, u32[]{:S(2)}) copy-start(f32[12,128,128]{2,1,0:T(8,128)} %param.16) | copy-start | bytes 2359300
  6.5 9.2 %copy-start.4 = (f32[1,128,128]{2,1,0:T(8,128)S(1)}, f32[1,128,128]{2,1,0:T(8,128)}, u32[]{:S(2)}) copy-start(f32[1,128,128]{2,1,0:T(8,128)} %param.17) | copy-start | bytes 196612
  6.5 70.6 %all-reduce.3.cloned.1.call-start = ((), (), s32[]{:S(2)}) async-start(), calls=%async_computation | async-start | bytes 262144 | tf_op jit(solution)/shard_map/psum | solution.py:40
  14.3 72.9 %copy-start.7 = (s32[12,4]{0,1:T(4,128)S(1)}, s32[12,4]{0,1:T(4,128)}, u32[]{:S(2)}) copy-start(s32[12,4]{0,1:T(4,128)} %param.23) | copy-start | bytes 580
  14.3 73.8 %copy-start.8 = (s32[1,2]{1,0:T(1,128)S(1)}, s32[1,2]{1,0:T(1,128)}, u32[]{:S(2)}) copy-start(s32[1,2]{1,0:T(1,128)} %param.24) | copy-start | bytes 28
  15.7 1.0 copy-start.1
  16.7 94.4 %all-gather.6.cloned.1.call-start = ((), (), s32[]{:S(2)}) async-start(), calls=%async_computation.3 | async-start | bytes 1179648 | tf_op jit(solution)/shard_map/all_gather | solution.py:39
  17.4 137.5 %all-gather.4.cloned.1.call-start = ((), (), s32[]{:S(2)}) async-start(), calls=%async_computation.1 | async-start | bytes 2228224 | tf_op jit(solution)/shard_map/all_gather | solution.py:43
  78.8 135.9 %all-reduce.5.cloned.1.call-start = ((), (), s32[]{:S(2)}) async-start(), calls=%async_computation.2 | async-start | bytes 262144 | tf_op jit(solution)/shard_map/psum | solution.py:46
  81.0 11.1 %collective-permute-start = (f32[2,256,256]{2,1,0:T(8,128)}, f32[2,256,256]{2,1,0:T(8,128)S(1)}, u32[]{:S(2)}, u32[]{:S(2)}) collective-permute-start(f32[2,256,256]{2,1,0:T(8,128)} %get-tuple-element.16), channel_id=1, source_target_pairs={{0,1},{1,2},{2,3},{3,4},{4,5},{5,6},{6,7},{7,8},{8,9},{9,10},{10,1... | collective-permute-start | bytes 1572872 | tf_op jit(solution)/shard_map/ppermute | solution.py:15
  84.6 12.3 %collective-permute-start.1 = (f32[2,256,256]{2,1,0:T(8,128)S(1)}, f32[2,256,256]{2,1,0:T(8,128)S(1)}, u32[]{:S(2)}, u32[]{:S(2)}) collective-permute-start(f32[2,256,256]{2,1,0:T(8,128)S(1)} %get-tuple-element.17), channel_id=1, source_target_pairs={{1,0},{2,1},{3,2},{4,3},{5,4},{6,5},{7,6},{8,7},{9,8},{10,9},{11,1... | collective-permute-start | bytes 1572872 | tf_op jit(solution)/shard_map/ppermute | solution.py:15
  101.1 53.9 %copy-start.5 = (f32[1,1,128,128]{3,2,1,0:T(8,128)S(1)}, f32[1,1,128,128]{3,2,1,0:T(8,128)}, u32[]{:S(2)}) copy-start(f32[1,1,128,128]{3,2,1,0:T(8,128)} %param.19) | copy-start | bytes 196612
  111.0 45.9 %copy-start.3 = (f32[1,2,128,128]{3,2,1,0:T(8,128)S(1)}, f32[1,2,128,128]{3,2,1,0:T(8,128)}, u32[]{:S(2)}) copy-start(f32[1,2,128,128]{3,2,1,0:T(8,128)} %param.18) | copy-start | bytes 393220
  111.0 103.8 %copy-start.6 = (f32[1,128,128]{2,1,0:T(8,128)S(1)}, f32[1,128,128]{2,1,0:T(8,128)}, u32[]{:S(2)}) copy-start(f32[1,128,128]{2,1,0:T(8,128)} %param.20) | copy-start | bytes 196612
Sparse Core Ops, SparseCore 0:
  16.8 60.3 all-reduce.2
  78.9 29.7 all-gather.5
  111.1 43.7 all-gather.3
  157.2 57.5 all-reduce.4
where the time goes:
time: 260 us; the launch traced here: 259 us
  waiting for transfers between devices  168 us (65%)
  matrix products  46.2 us (18%)
  local copies, waits for them, and re-layouts  19.6 us (8%)
  between operations  14 us (5%)
  starting transfers between devices  6.29 us (2%)
  other arithmetic  4.21 us (2%)
    psum x1, waiting for transfers between devices, shards(): group_coeffs = lax.psum(up_term, 'narrow')  59.7 us
    psum x1, waiting for transfers between devices, shards(): group_out = lax.psum(partial_value, 'narrow')  57.3 us
    all_gather x1, waiting for transfers between devices, shards(): all_groups = lax.all_gather(group_coeffs[None], 'wide', axis=0, tiled=True)  41.7 us
    dot_general x1, matrix products, shards(): jnp.einsum('ljpq,ljpv->lqv', near_blocks, sources, precision=HIGH)  27 us
    gather x1, local copies, waits for them, and re-layouts, shards(): sources = extended[local_index]  9.96 us
    ppermute x2, waiting for transfers between devices, from_behind(): lax.ppermute(value, axis, [(source, source + steps) for source in range(l...  8.8 us
    dot_general x1, matrix products, shards(): jnp.einsum('lpk,lpv->lkv', row_basis, cotangent, precision=HIGH)  7.7 us
    ppermute x2, starting transfers between devices, from_behind(): lax.ppermute(value, axis, [(source, source + steps) for source in range(l...  6.17 us
  transfers between devices with their start and end apart: 6, of which 5 were waited for; matrix products, arithmetic and copies ran while one was open for 8% of the time, Pallas kernels for 0%

commit v1 on v0

v1 whole, which is shorter than its diff:
```python
import functools

import jax
import jax.numpy as jnp
from jax import lax
from jax.experimental import pallas as pl
from jax.experimental.pallas import tpu as pltpu
from jax.sharding import PartitionSpec as P

MESH = pl.DeviceIdType.MESH
F32, BF16 = jnp.float32, jnp.bfloat16
LEAVES, PTS, RANK, NVEC = 12, 256, 128, 256
REACH, NNEAR = 2, 4
WIDE, NARROW, SIDE = 16, 8, 4
SLICE = NVEC // NARROW
OFFSETS = [(dz, dx) for dz in (2, 1, 3, 0) for dx in (2, 1, 3, 0) if dz or dx]


def split(value):
    high = value.astype(BF16)
    return high, (value - high.astype(F32)).astype(BF16)


def dot(a, b, dims=((1,), (0,))):
    return lax.dot_general(a, b, (dims, ((), ())), preferred_element_type=F32)


def dot3(a, b, dims=((1,), (0,))):
    (ah, al), (bh, bl) = a, b
    return dot(ah, bh, dims) + (dot(al, bh, dims) + dot(ah, bl, dims))


def exchange(
    cot, rb, cb, lu, nu, nc, gc, nd, ld, nb, ni_hbm, fn_hbm, fg,
    near_out, mh_out, ml_out, nth_out, ntl_out,
    cotv, rbv, cbv, luv, nuv, ncv, gcv, ndv, ldv, nbv,
    cth, ctl, upv, sib, abuf, bbuf, cbuf, outv, ni, fn,
    leaf_sem, small_sem, cb_sem, nb_sem,
    sa, ra, sb, rb_, sc, rc, ss, rs, sg, rg, sh, rh, go, int_sem,
):
    w, n = lax.axis_index("wide"), lax.axis_index("narrow")
    core = lax.rem(n, 2)

    def mate(d):
        return w, lax.rem(n + d, NARROW)

    def far(dz, dx, sign):
        z = lax.rem(w // SIDE + SIDE + sign * dz, SIDE)
        x = lax.rem(lax.rem(w, SIDE) + SIDE + sign * dx, SIDE)
        return z * SIDE + x, n

    rank = w * NARROW + n
    after, before = lax.rem(rank + 1, WIDE * NARROW), lax.rem(rank + WIDE * NARROW - 1, WIDE * NARROW)
    after, before = (after // NARROW, lax.rem(after, NARROW)), (before // NARROW, lax.rem(before, NARROW))

    barrier = pltpu.get_barrier_semaphore()
    for dz, dx in OFFSETS:
        pl.semaphore_signal(barrier, inc=1, device_id=far(dz, dx, 1), device_id_type=MESH)
    for d in range(1, NARROW):
        pl.semaphore_signal(barrier, inc=1, device_id=mate(d), device_id_type=MESH)

    def leaf_copies(leaf):
        return [
            pltpu.make_async_copy(rb.at[leaf], rbv.at[leaf], leaf_sem.at[0, leaf]),
            pltpu.make_async_copy(lu.at[leaf], luv.at[leaf], leaf_sem.at[1, leaf]),
            pltpu.make_async_copy(cot.at[leaf], cotv.at[REACH + leaf], leaf_sem.at[2, leaf]),
        ]

    @pl.loop(0, LEAVES)
    def _(leaf):
        for c in leaf_copies(leaf):
            c.start()

    smalls = [
        pltpu.make_async_copy(nu.at[0], nuv, small_sem.at[0]),
        pltpu.make_async_copy(gc.at[0, 0], gcv.at[n, pl.ds(0, RANK)], small_sem.at[1]),
        pltpu.make_async_copy(nc.at[0], ncv, small_sem.at[2]),
        pltpu.make_async_copy(nd.at[0], ndv, small_sem.at[3]),
    ]
    ints = [
        pltpu.make_async_copy(a, b, int_sem.at[i])
        for i, (a, b) in enumerate(((ni_hbm, ni), (fn_hbm, fn)))
    ]
    for c in smalls + ints:
        c.start()
    for c in ints:
        c.wait()

    gcv[n, RANK:, :] = jnp.full((8, RANK), fg[0, 0].astype(F32), F32)
    upv[...] = jnp.zeros_like(upv)

    def prepare(slot):
        turned = cotv[slot].T
        high, low = split(turned)
        cth[slot], ctl[slot] = high, low
        return high, low

    @pl.loop(0, LEAVES)
    def _(leaf):
        for c in leaf_copies(leaf):
            c.wait()
        basis = dot3(split(rbv[leaf]), split(luv[leaf]))
        upv[...] += dot3(prepare(REACH + leaf), split(basis))

    near_copies = functools.partial(
        lambda leaf: pltpu.make_async_copy(nb.at[leaf], nbv.at[leaf], nb_sem.at[leaf])
    )
    late = [pltpu.make_async_copy(cb, cbv, cb_sem.at[0]), pltpu.make_async_copy(ld, ldv, cb_sem.at[1])]
    for c in late:
        c.start()

    @pl.loop(0, LEAVES)
    def _(leaf):
        near_copies(leaf).start()

    coeffs = upv[...]
    sib[n] = coeffs
    for c in smalls:
        c.wait()
    upv[...] = dot3(split(coeffs), split(nuv[...]))

    pl.semaphore_wait(barrier, len(OFFSETS) + NARROW - 1)

    first = []
    for d in range(1, NARROW):
        to = mate(d)
        first.append(
            pltpu.make_async_remote_copy(
                upv.at[pl.ds(pl.multiple_of(to[1] * SLICE, SLICE), SLICE)], abuf.at[d - 1],
                sa.at[d - 1], ra.at[d - 1], device_id=to, device_id_type=MESH,
            )
        )
        first[-1].start()

    @pl.when(n == NARROW - 1)
    def _():
        pl.semaphore_signal(go, inc=1, device_id=(lax.rem(w + WIDE - 1, WIDE), n), device_id_type=MESH)

    @pl.when(n == 0)
    def _():
        pl.semaphore_signal(go, inc=1, device_id=(lax.rem(w + 1, WIDE), n), device_id_type=MESH)

    twin = (w, n + 1 - 2 * core)

    def spread(buf, send, recv):
        out = []
        for step in range(SIDE):
            to = twin if step == 0 else mate(2 * step)
            out.append(
                pltpu.make_async_remote_copy(
                    buf.at[n], buf.at[n], send.at[step], recv.at[step], device_id=to, device_id_type=MESH
                )
            )
        return out

    def arrived(buf, send, recv, step):
        source = lax.rem(n + NARROW - 2 * step, NARROW)
        return pltpu.make_async_remote_copy(
            buf.at[source], buf.at[source], send.at[step], recv.at[step], device_id=twin, device_id_type=MESH
        )

    def relay(buf, send, recv, step):
        source = lax.rem(n + NARROW - 2 * step, NARROW)
        return pltpu.make_async_remote_copy(
            buf.at[source], buf.at[source], send.at[SIDE - 1 + step], recv.at[SIDE - 1 + step],
            device_id=twin, device_id_type=MESH,
        )

    groups = spread(gcv, sg, rg)
    for c in groups:
        c.start()
    siblings = spread(sib, ss, rs)
    for c in siblings:
        c.start()

    @pl.when((n == NARROW - 1) | (n == 0))
    def _():
        pl.semaphore_wait(go, 1)

    halo = [
        pltpu.make_async_remote_copy(
            cot.at[pl.ds(LEAVES - REACH, REACH)], cotv.at[pl.ds(0, REACH)],
            sh.at[0], rh.at[0], device_id=after, device_id_type=MESH,
        ),
        pltpu.make_async_remote_copy(
            cot.at[pl.ds(0, REACH)], cotv.at[pl.ds(REACH + LEAVES, REACH)],
            sh.at[1], rh.at[1], device_id=before, device_id_type=MESH,
        ),
    ]
    for c in halo:
        c.start()

    for c in late:
        c.wait()

    @pl.loop(0, LEAVES)
    def _(leaf):
        mh, ml = split(dot3(split(cbv[leaf]), split(ldv[leaf])))
        mh_out[leaf], ml_out[leaf] = mh, ml

    first_leaf = rank * LEAVES - REACH

    def near(leaf):
        near_copies(leaf).wait()
        total = None
        for j in range(NNEAR):
            source = jnp.clip(ni[j, leaf] - first_leaf, 0, LEAVES + 2 * REACH - 1)
            term = dot3((cth[source], ctl[source]), split(nbv[leaf, j]))
            total = term if total is None else total + term
        near_out[leaf] = total.T

    @pl.loop(2, 5)
    def _(leaf):
        near(leaf)

    own = upv[pl.ds(pl.multiple_of(n * SLICE, SLICE), SLICE), :]
    for d, c in enumerate(first):
        c.wait_recv()
        own += abuf[d]
    bbuf[w] = own
    second = []
    for i, (dz, dx) in enumerate(OFFSETS):
        second.append(
            pltpu.make_async_remote_copy(
                bbuf.at[w], bbuf.at[w], sb.at[i], rb_.at[i], device_id=far(dz, dx, 1), device_id_type=MESH
            )
        )
        second[-1].start()

    relays = []
    for step in range(1, SIDE):
        arrived(gcv, sg, rg, step).wait_recv()
        relays.append(relay(gcv, sg, rg, step))
        relays[-1].start()

    @pl.loop(5, 10)
    def _(leaf):
        near(leaf)

    for step in range(1, SIDE):
        arrived(sib, ss, rs, step).wait_recv()
        relays.append(relay(sib, ss, rs, step))
        relays[-1].start()

    def from_twin(buf, send, recv, step):
        at = 0 if step == 0 else SIDE - 1 + step
        source = lax.rem(twin[1] + NARROW - 2 * step, NARROW)
        return pltpu.make_async_remote_copy(
            buf.at[source], buf.at[source], send.at[at], recv.at[at], device_id=twin, device_id_type=MESH
        )

    for step in range(SIDE):
        from_twin(gcv, sg, rg, step).wait_recv()
    for i, (dz, dx) in enumerate(OFFSETS):
        source = far(dz, dx, -1)[0]
        pltpu.make_async_remote_copy(
            bbuf.at[source], bbuf.at[source], sb.at[i], rb_.at[i], device_id=far(dz, dx, 1), device_id_type=MESH
        ).wait_recv()

    part = jnp.zeros((SLICE, RANK), F32)
    for j in range(NARROW):
        tag = jnp.concatenate([gcv[j, RANK:, :]] * (SLICE // 8), axis=0)
        picked = bbuf[0]
        for g in range(1, WIDE):
            picked = jnp.where(tag == float(g), bbuf[g], picked)
        part += dot3(split(picked), split(gcv[j, :RANK, :]))
    mine = pl.ds(pl.multiple_of(n * SLICE, SLICE), SLICE)
    cbuf[mine, :] = part
    third = []
    for d in range(1, NARROW):
        third.append(
            pltpu.make_async_remote_copy(
                cbuf.at[mine], cbuf.at[mine], sc.at[d - 1], rc.at[d - 1], device_id=mate(d), device_id_type=MESH
            )
        )
        third[-1].start()

    for step in range(SIDE):
        from_twin(sib, ss, rs, step).wait_recv()
    node = jnp.zeros((NVEC, RANK), F32)
    for j in range(2):
        node += dot3(split(sib[jnp.clip(fn[0, j], 0, NARROW - 1)]), split(ncv[j]))
    outv[...] = node

    for c in halo:
        c.wait_recv()
    for slot in (0, 1, REACH + LEAVES, REACH + LEAVES + 1):
        prepare(slot)

    @pl.loop(0, 4)
    def _(i):
        near(i + jnp.where(i < 2, 0, LEAVES - 4))

    for d in range(1, NARROW):
        source = pl.ds(pl.multiple_of(lax.rem(n + NARROW - d, NARROW) * SLICE, SLICE), SLICE)
        pltpu.make_async_remote_copy(
            cbuf.at[source], cbuf.at[source], sc.at[d - 1], rc.at[d - 1], device_id=mate(d), device_id_type=MESH
        ).wait_recv()
    node = outv[...] + dot3(split(cbuf[...]), split(ndv[...]), ((1,), (1,)))
    nth_out[...], ntl_out[...] = split(node.T)

    for c in first + second + third + groups + siblings + relays + halo:
        c.wait_send()


def finish(near, mh, ml, nth, ntl, out, buf, sem):
    def done(leaf):
        return pltpu.make_async_copy(buf.at[leaf], out.at[leaf], sem.at[leaf])

    @pl.loop(0, LEAVES)
    def _(leaf):
        buf[leaf] = near[leaf] + dot3((mh[leaf], ml[leaf]), (nth[...], ntl[...]))
        done(leaf).start()

    @pl.loop(0, LEAVES)
    def _(leaf):
        done(leaf).wait()


def shards(cot, rb, cb, lu, nu, nc, gc, nd, ld, nb, ni, fn, fg):
    hbm = pl.BlockSpec(memory_space=pltpu.HBM)
    vmem = pl.BlockSpec(memory_space=pltpu.VMEM)
    dma = pltpu.SemaphoreType.DMA
    shape = jax.ShapeDtypeStruct
    parts = pl.pallas_call(
        exchange,
        out_shape=[
            pltpu.VMEM((LEAVES, PTS, NVEC), F32),
            pltpu.VMEM((LEAVES, PTS, RANK), BF16),
            pltpu.VMEM((LEAVES, PTS, RANK), BF16),
            pltpu.VMEM((RANK, NVEC), BF16),
            pltpu.VMEM((RANK, NVEC), BF16),
        ],
        in_specs=[hbm] * 12 + [pl.BlockSpec(memory_space=pltpu.SMEM)],
        out_specs=[vmem] * 5,
        scratch_shapes=[
            pltpu.VMEM((LEAVES + 2 * REACH, PTS, NVEC), F32),
            pltpu.VMEM((LEAVES, PTS, RANK), F32),
            pltpu.VMEM((LEAVES, PTS, RANK), F32),
            pltpu.VMEM((LEAVES, RANK, RANK), F32),
            pltpu.VMEM((RANK, RANK), F32),
            pltpu.VMEM((2, RANK, RANK), F32),
            pltpu.VMEM((NARROW, RANK + 8, RANK), F32),
            pltpu.VMEM((RANK, RANK), F32),
            pltpu.VMEM((LEAVES, RANK, RANK), F32),
            pltpu.VMEM((LEAVES, NNEAR, PTS, PTS), F32),
            pltpu.VMEM((LEAVES + 2 * REACH, NVEC, PTS), BF16),
            pltpu.VMEM((LEAVES + 2 * REACH, NVEC, PTS), BF16),
            pltpu.VMEM((NVEC, RANK), F32),
            pltpu.VMEM((NARROW, NVEC, RANK), F32),
            pltpu.VMEM((NARROW - 1, SLICE, RANK), F32),
            pltpu.VMEM((WIDE, SLICE, RANK), F32),
            pltpu.VMEM((NVEC, RANK), F32),
            pltpu.VMEM((NVEC, RANK), F32),
            pltpu.SMEM((NNEAR, LEAVES), jnp.int32),
            pltpu.SMEM((1, 2), jnp.int32),
            dma((3, LEAVES)),
            dma((4,)),
            dma((2,)),
            dma((LEAVES,)),
            dma((NARROW - 1,)),
            dma((NARROW - 1,)),
            dma((WIDE - 1,)),
            dma((WIDE - 1,)),
            dma((NARROW - 1,)),
            dma((NARROW - 1,)),
            dma((2 * SIDE - 1,)),
            dma((2 * SIDE - 1,)),
            dma((2 * SIDE - 1,)),
            dma((2 * SIDE - 1,)),
            dma((2,)),
            dma((2,)),
            pltpu.SemaphoreType.REGULAR,
            dma((2,)),
        ],
        compiler_params=pltpu.CompilerParams(
            collective_id=0, has_side_effects=True, vmem_limit_bytes=48 * 2**20
        ),
    )(*[pltpu.with_memory_space_constraint(a, pltpu.HBM) for a in (cot, rb, cb, lu, nu, nc, gc, nd, ld, nb, ni.T, fn)], fg)
    return pl.pallas_call(
        finish,
        out_shape=shape((LEAVES, PTS, NVEC), F32),
        in_specs=[vmem] * 5,
        out_specs=hbm,
        scratch_shapes=[pltpu.VMEM((LEAVES, PTS, NVEC), F32), dma((LEAVES,))],
        compiler_params=pltpu.CompilerParams(vmem_limit_bytes=24 * 2**20),
    )(*parts)


def solution(mesh):
    leaf, both = P(("wide", "narrow"), None, None), P(("wide", "narrow"), None)
    wide4 = P(("wide", "narrow"), None, None, None)
    in_specs = (
        leaf, leaf, leaf, leaf, leaf, wide4, P("wide", "narrow", None, None), leaf, leaf, wide4,
        both, both, P("wide", "narrow"),
    )
    return jax.shard_map(shards, mesh=mesh, in_specs=in_specs, out_specs=leaf, check_vma=False)
```

time: 260 us -> 42 us (0.16)
  waiting for transfers between devices: 168 us -> 0 us
  matrix products: 46.2 us -> 0 us
  Pallas kernels: 0 us -> 41.3 us
  local copies, waits for them, and re-layouts: 19.6 us -> 0 us
  between operations: 14 us -> 0.66 us
  starting transfers between devices: 6.29 us -> 0 us
  other arithmetic: 4.21 us -> 0 us
    psum x2 -> x0, waiting for transfers between devices: 117 us -> none  [the longest x1 59.7 us: shards(): group_coeffs = lax.psum(up_term, 'narrow')]
    dot_general x9 -> x0, matrix products: 46.2 us -> none  [the longest x1 27 us: shards(): jnp.einsum('ljpq,ljpv->lqv', near_blocks, sources, precision=HIGH)]
    all_gather x2 -> x0, waiting for transfers between devices: 41.7 us -> none  [the longest x1 41.7 us: shards(): all_groups = lax.all_gather(group_coeffs[None], 'wide', axis=0, tiled=True)]
    pallas_call x0 -> x2, Pallas kernels: none -> 41.3 us  [the longest x1 37.5 us: shards(): pl.pallas_call(exchange, out_shape=[pltpu.VMEM((LEAVES, PTS, NVEC), F32),...]
    gather x2 -> x0, local copies, waits for them, and re-layouts: 10.5 us -> none  [the longest x1 9.96 us: shards(): sources = extended[local_index]]
    ppermute x2 -> x0, waiting for transfers between devices: 8.8 us -> none  [from_behind(): lax.ppermute(value, axis, [(source, source + steps) for source in range(l...]
    ppermute x2 -> x0, starting transfers between devices: 6.17 us -> none  [from_behind(): lax.ppermute(value, axis, [(source, source + steps) for source in range(l...]
    concatenate x1 -> x0, other arithmetic: 4.18 us -> none  [shards(): extended = jnp.concatenate([lower, cotangent, upper], axis=0)]
  transfers between devices with their start and end apart: 6 -> 0, of which waited for: 5 -> 0; matrix products, arithmetic and copies ran while one was open for 8% -> 0% of each run, Pallas kernels for 0% -> 0%
where the time goes in v1:
time: 42 us; the launch traced here: 41.9 us
  Pallas kernels  41.3 us (98%)
  between operations  0.66 us (2%)
    pallas_call x1, Pallas kernels, shards(): pl.pallas_call(exchange, out_shape=[pltpu.VMEM((LEAVES, PTS, NVEC), F32),...  37.5 us
    pallas_call x1, Pallas kernels, shards(): pl.pallas_call(finish, out_shape=shape((LEAVES, PTS, NVEC), F32), in_spec...  3.79 us

profile of v1, /device:TPU:1, one launch (start us, length us, event | category | flops | bytes accessed | tf_op | source)
XLA Modules:
  0.0 41.9 jit_solution(9778224033843500481)
XLA Ops:
  0.7 37.5 %shard_map.127 = (f32[12,256,256]{2,1,0:T(8,128)S(1)}, bf16[12,256,128]{2,1,0:T(8,128)(2,1)S(1)}, bf16[12,256,128]{2,1,0:T(8,128)(2,1)S(1)}, bf16[128,256]{1,0:T(8,128)(2,1)S(1)}, bf16[128,256]{1,0:T(8,128)(2,1)S(1)}) custom-call(f32[12,256,256]{2,1,0:T(8,128)} %cot.1, f32[12,256,128]{2,1,0:T(8,128)} %rb.1, f32[12,256,128]{2,1,0:T(8,128)} %cb.1, ...), custom_call_target="tpu_custom_call" | custom-call | tf_op jit(solution)/shard_map/pallas_call | solution.py:325
  38.1 3.8 %shard_map.128 = f32[12,256,256]{2,1,0:T(8,128)} custom-call(f32[12,256,256]{2,1,0:T(8,128)S(1)} %get-tuple-element.10.near, bf16[12,256,128]{2,1,0:T(8,128)(2,1)S(1)} %get-tuple-element.11.mh, bf16[12,256,128]{2,1,0:T(8,128)(2,1)S(1)} %get-tuple-element.12.ml, bf16[128,256]{1,0:T(8,128)(2,1)S(1)} %get-tuple-element.13.nth, ...), custom_call_target="tpu_custom_call" | custom-call | tf_op jit(solution)/shard_map/pallas_call | solution.py:380

commit v2 on v1

--- a/solution.py
+++ b/solution.py
@@ -11,6 +11,11 @@
 F32, BF16 = jnp.float32, jnp.bfloat16
 LEAVES, PTS, RANK, NVEC = 12, 256, 128, 256
 REACH, NNEAR = 2, 4
+PIECES = 4
+CHUNK = 3
+CHUNKS = LEAVES // CHUNK
+AHEAD = 3
+PIECE = PTS // PIECES
 WIDE, NARROW, SIDE = 16, 8, 4
 SLICE = NVEC // NARROW
 OFFSETS = [(dz, dx) for dz in (2, 1, 3, 0) for dx in (2, 1, 3, 0) if dz or dx]
@@ -32,11 +37,11 @@
 
 def exchange(
     cot, rb, cb, lu, nu, nc, gc, nd, ld, nb, ni_hbm, fn_hbm, fg,
-    near_out, mh_out, ml_out, nth_out, ntl_out,
+    near_out, mm_out, nt_out,
     cotv, rbv, cbv, luv, nuv, ncv, gcv, ndv, ldv, nbv,
-    cth, ctl, upv, sib, abuf, bbuf, cbuf, outv, ni, fn,
+    cth, ctl, up_sum, upv, sib, abuf, bbuf, cbuf, outv, ni, fn,
     leaf_sem, small_sem, cb_sem, nb_sem,
-    sa, ra, sb, rb_, sc, rc, ss, rs, sg, rg, sh, rh, go, int_sem,
+    sa, ra, sb, rb_, sc, rc, ss, rs, sg, rg, sh, rh, int_sem,
 ):
     w, n = lax.axis_index("wide"), lax.axis_index("narrow")
     core = lax.rem(n, 2)
@@ -58,17 +63,23 @@
         pl.semaphore_signal(barrier, inc=1, device_id=far(dz, dx, 1), device_id_type=MESH)
     for d in range(1, NARROW):
         pl.semaphore_signal(barrier, inc=1, device_id=mate(d), device_id_type=MESH)
-
-    def leaf_copies(leaf):
+    for to in (after, before):
+        pl.semaphore_signal(barrier, inc=1, device_id=to, device_id_type=MESH)
+
+    def chunk_copies(chunk):
+        at = pl.ds(chunk * CHUNK, CHUNK)
         return [
-            pltpu.make_async_copy(rb.at[leaf], rbv.at[leaf], leaf_sem.at[0, leaf]),
-            pltpu.make_async_copy(lu.at[leaf], luv.at[leaf], leaf_sem.at[1, leaf]),
-            pltpu.make_async_copy(cot.at[leaf], cotv.at[REACH + leaf], leaf_sem.at[2, leaf]),
+            pltpu.make_async_copy(rb.at[at], rbv.at[at], leaf_sem.at[0, chunk]),
+            pltpu.make_async_copy(lu.at[at], luv.at[at], leaf_sem.at[1, chunk]),
+            pltpu.make_async_copy(cot.at[at], cotv.at[pl.ds(REACH + chunk * CHUNK, CHUNK)], leaf_sem.at[2, chunk]),
         ]
 
-    @pl.loop(0, LEAVES)
-    def _(leaf):
-        for c in leaf_copies(leaf):
+    def near_copy(i):
+        leaf = lax.rem(i + REACH, LEAVES)
+        return pltpu.make_async_copy(nb.at[leaf], nbv.at[leaf], nb_sem.at[leaf])
+
+    for chunk in range(2):
+        for c in chunk_copies(chunk):
             c.start()
 
     smalls = [
@@ -87,39 +98,54 @@
         c.wait()
 
     gcv[n, RANK:, :] = jnp.full((8, RANK), fg[0, 0].astype(F32), F32)
-    upv[...] = jnp.zeros_like(upv)
+    up_sum[...] = jnp.zeros_like(up_sum)
 
     def prepare(slot):
-        turned = cotv[slot].T
-        high, low = split(turned)
-        cth[slot], ctl[slot] = high, low
-        return high, low
-
-    @pl.loop(0, LEAVES)
-    def _(leaf):
-        for c in leaf_copies(leaf):
+        cth[slot], ctl[slot] = split(cotv[slot].T)
+
+    late = [pltpu.make_async_copy(cb, cbv, cb_sem.at[0]), pltpu.make_async_copy(ld, ldv, cb_sem.at[1])]
+
+    @pl.loop(0, CHUNKS)
+    def _(chunk):
+        for c in chunk_copies(chunk):
             c.wait()
-        basis = dot3(split(rbv[leaf]), split(luv[leaf]))
-        upv[...] += dot3(prepare(REACH + leaf), split(basis))
-
-    near_copies = functools.partial(
-        lambda leaf: pltpu.make_async_copy(nb.at[leaf], nbv.at[leaf], nb_sem.at[leaf])
-    )
-    late = [pltpu.make_async_copy(cb, cbv, cb_sem.at[0]), pltpu.make_async_copy(ld, ldv, cb_sem.at[1])]
-    for c in late:
-        c.start()
-
-    @pl.loop(0, LEAVES)
-    def _(leaf):
-        near_copies(leaf).start()
-
-    coeffs = upv[...]
+
+        @pl.when(chunk < CHUNKS - 2)
+        def _():
+            for c in chunk_copies(chunk + 2):
+                c.start()
+
+        @pl.when(chunk == CHUNKS - 2)
+        def _():
+            for i in range(AHEAD):
+                near_copy(i).start()
+
+        @pl.when(chunk == CHUNKS - 1)
+        def _():
+            for c in late:
+                c.start()
+
+        total = None
+        for i in range(CHUNK):
+            leaf = chunk * CHUNK + i
+            lh, ll = split(luv[leaf].T)
+            bh, bl = split(rbv[leaf])
+            stacked = dot(jnp.concatenate([lh, ll], axis=0), bh, ((1,), (1,)))
+            basis = stacked[:RANK] + stacked[RANK:] + dot(lh, bl, ((1,), (1,)))
+            bh, bl = split(basis)
+            ch, cl = split(cotv[REACH + leaf])
+            stacked = dot(jnp.concatenate([bh, bl], axis=0), ch)
+            term = stacked[:RANK] + stacked[RANK:] + dot(bh, cl)
+            total = term if total is None else total + term
+        up_sum[...] += total
+
+    coeffs = up_sum[...].T
     sib[n] = coeffs
     for c in smalls:
         c.wait()
     upv[...] = dot3(split(coeffs), split(nuv[...]))
 
-    pl.semaphore_wait(barrier, len(OFFSETS) + NARROW - 1)
+    pl.semaphore_wait(barrier, len(OFFSETS) + NARROW + 1)
 
     first = []
     for d in range(1, NARROW):
@@ -131,14 +157,6 @@
             )
         )
         first[-1].start()
-
-    @pl.when(n == NARROW - 1)
-    def _():
-        pl.semaphore_signal(go, inc=1, device_id=(lax.rem(w + WIDE - 1, WIDE), n), device_id_type=MESH)
-
-    @pl.when(n == 0)
-    def _():
-        pl.semaphore_signal(go, inc=1, device_id=(lax.rem(w + 1, WIDE), n), device_id_type=MESH)
 
     twin = (w, n + 1 - 2 * core)
 
@@ -167,41 +185,55 @@
         )
 
     groups = spread(gcv, sg, rg)
+    siblings = spread(sib, ss, rs)
+
+    def halo(i):
+        leaf, rows = i // PIECES, pl.ds(pl.multiple_of(lax.rem(i, PIECES) * PIECE, PIECE), PIECE)
+        return [
+            pltpu.make_async_remote_copy(
+                cot.at[LEAVES - REACH + leaf, rows], cotv.at[leaf, rows],
+                sh.at[0, i], rh.at[0, i], device_id=after, device_id_type=MESH,
+            ),
+            pltpu.make_async_remote_copy(
+                cot.at[leaf, rows], cotv.at[REACH + LEAVES + leaf, rows],
+                sh.at[1, i], rh.at[1, i], device_id=before, device_id_type=MESH,
+            ),
+        ]
+
+    def send_halo(low, high):
+        @pl.loop(low, high)
+        def _(i):
+            for c in halo(i):
+                c.start()
+
+    def merge_down():
+        for c in late:
+            c.wait()
+
+        @pl.loop(0, LEAVES, unroll=2)
+        def _(leaf):
+            wh, wl = split(ldv[leaf])
+            row = jnp.concatenate([wh, wl], axis=1)
+            both = dot(jnp.concatenate(split(cbv[leaf]), axis=1), jnp.concatenate([row, row], axis=0))
+            mm_out[leaf] = jnp.concatenate(split(both[:, :RANK] + both[:, RANK:]), axis=1)
+
     for c in groups:
         c.start()
-    siblings = spread(sib, ss, rs)
-    for c in siblings:
-        c.start()
-
-    @pl.when((n == NARROW - 1) | (n == 0))
-    def _():
-        pl.semaphore_wait(go, 1)
-
-    halo = [
-        pltpu.make_async_remote_copy(
-            cot.at[pl.ds(LEAVES - REACH, REACH)], cotv.at[pl.ds(0, REACH)],
-            sh.at[0], rh.at[0], device_id=after, device_id_type=MESH,
-        ),
-        pltpu.make_async_remote_copy(
-            cot.at[pl.ds(0, REACH)], cotv.at[pl.ds(REACH + LEAVES, REACH)],
-            sh.at[1], rh.at[1], device_id=before, device_id_type=MESH,
-        ),
-    ]
-    for c in halo:
-        c.start()
-
-    for c in late:
-        c.wait()
-
-    @pl.loop(0, LEAVES)
+
+    @pl.loop(0, LEAVES, unroll=2)
     def _(leaf):
-        mh, ml = split(dot3(split(cbv[leaf]), split(ldv[leaf])))
-        mh_out[leaf], ml_out[leaf] = mh, ml
+        prepare(REACH + leaf)
 
     first_leaf = rank * LEAVES - REACH
 
-    def near(leaf):
-        near_copies(leaf).wait()
+    def near(i):
+        leaf = lax.rem(i + REACH, LEAVES)
+        near_copy(i).wait()
+
+        @pl.when(i + AHEAD < LEAVES)
+        def _():
+            near_copy(i + AHEAD).start()
+
         total = None
         for j in range(NNEAR):
             source = jnp.clip(ni[j, leaf] - first_leaf, 0, LEAVES + 2 * REACH - 1)
@@ -209,9 +241,11 @@
             total = term if total is None else total + term
         near_out[leaf] = total.T
 
-    @pl.loop(2, 5)
+    @pl.loop(0, 2)
     def _(leaf):
         near(leaf)
+
+    merge_down()
 
     own = upv[pl.ds(pl.multiple_of(n * SLICE, SLICE), SLICE), :]
     for d, c in enumerate(first):
@@ -233,7 +267,12 @@
         relays.append(relay(gcv, sg, rg, step))
         relays[-1].start()
 
-    @pl.loop(5, 10)
+    send_halo(0, 8)
+
+    for c in siblings:
+        c.start()
+
+    @pl.loop(2, 8)
     def _(leaf):
         near(leaf)
 
@@ -282,14 +321,17 @@
         node += dot3(split(sib[jnp.clip(fn[0, j], 0, NARROW - 1)]), split(ncv[j]))
     outv[...] = node
 
-    for c in halo:
-        c.wait_recv()
+    @pl.loop(0, REACH * PIECES)
+    def _(i):
+        for c in halo(i):
+            c.wait_recv()
+
     for slot in (0, 1, REACH + LEAVES, REACH + LEAVES + 1):
         prepare(slot)
 
-    @pl.loop(0, 4)
+    @pl.loop(LEAVES - 2 * REACH, LEAVES)
     def _(i):
-        near(i + jnp.where(i < 2, 0, LEAVES - 4))
+        near(i)
 
     for d in range(1, NARROW):
         source = pl.ds(pl.multiple_of(lax.rem(n + NARROW - d, NARROW) * SLICE, SLICE), SLICE)
@@ -297,19 +339,26 @@
             cbuf.at[source], cbuf.at[source], sc.at[d - 1], rc.at[d - 1], device_id=mate(d), device_id_type=MESH
         ).wait_recv()
     node = outv[...] + dot3(split(cbuf[...]), split(ndv[...]), ((1,), (1,)))
-    nth_out[...], ntl_out[...] = split(node.T)
-
-    for c in first + second + third + groups + siblings + relays + halo:
+    high, low = split(node.T)
+    nt_out[0:RANK], nt_out[RANK : 2 * RANK], nt_out[2 * RANK :] = high, high, low
+
+    for c in first + second + third + groups + siblings + relays:
         c.wait_send()
 
-
-def finish(near, mh, ml, nth, ntl, out, buf, sem):
+    @pl.loop(0, REACH * PIECES)
+    def _(i):
+        for c in halo(i):
+            c.wait_send()
+
+
+def finish(near, mm, nt, out, buf, sem):
     def done(leaf):
         return pltpu.make_async_copy(buf.at[leaf], out.at[leaf], sem.at[leaf])
 
-    @pl.loop(0, LEAVES)
+    @pl.loop(0, LEAVES, unroll=2)
     def _(leaf):
-        buf[leaf] = near[leaf] + dot3((mh[leaf], ml[leaf]), (nth[...], ntl[...]))
+        far = dot(mm[leaf], nt[: 2 * RANK]) + dot(mm[leaf, :, :RANK], nt[2 * RANK :])
+        buf[leaf] = near[leaf] + far
         done(leaf).start()
 
     @pl.loop(0, LEAVES)
@@ -326,13 +375,11 @@
         exchange,
         out_shape=[
             pltpu.VMEM((LEAVES, PTS, NVEC), F32),
-            pltpu.VMEM((LEAVES, PTS, RANK), BF16),
-            pltpu.VMEM((LEAVES, PTS, RANK), BF16),
-            pltpu.VMEM((RANK, NVEC), BF16),
-            pltpu.VMEM((RANK, NVEC), BF16),
+            pltpu.VMEM((LEAVES, PTS, 2 * RANK), BF16),
+            pltpu.VMEM((3 * RANK, NVEC), BF16),
         ],
         in_specs=[hbm] * 12 + [pl.BlockSpec(memory_space=pltpu.SMEM)],
-        out_specs=[vmem] * 5,
+        out_specs=[vmem] * 3,
         scratch_shapes=[
             pltpu.VMEM((LEAVES + 2 * REACH, PTS, NVEC), F32),
             pltpu.VMEM((LEAVES, PTS, RANK), F32),
@@ -346,6 +393,7 @@
             pltpu.VMEM((LEAVES, NNEAR, PTS, PTS), F32),
             pltpu.VMEM((LEAVES + 2 * REACH, NVEC, PTS), BF16),
             pltpu.VMEM((LEAVES + 2 * REACH, NVEC, PTS), BF16),
+            pltpu.VMEM((RANK, NVEC), F32),
             pltpu.VMEM((NVEC, RANK), F32),
             pltpu.VMEM((NARROW, NVEC, RANK), F32),
             pltpu.VMEM((NARROW - 1, SLICE, RANK), F32),
@@ -354,7 +402,7 @@
             pltpu.VMEM((NVEC, RANK), F32),
             pltpu.SMEM((NNEAR, LEAVES), jnp.int32),
             pltpu.SMEM((1, 2), jnp.int32),
-            dma((3, LEAVES)),
+            dma((3, CHUNKS)),
             dma((4,)),
             dma((2,)),
             dma((LEAVES,)),
@@ -368,9 +416,8 @@
             dma((2 * SIDE - 1,)),
             dma((2 * SIDE - 1,)),
             dma((2 * SIDE - 1,)),
-            dma((2,)),
-            dma((2,)),
-            pltpu.SemaphoreType.REGULAR,
+            dma((2, REACH * PIECES)),
+            dma((2, REACH * PIECES)),
             dma((2,)),
         ],
         compiler_params=pltpu.CompilerParams(
@@ -380,7 +427,7 @@
     return pl.pallas_call(
         finish,
         out_shape=shape((LEAVES, PTS, NVEC), F32),
-        in_specs=[vmem] * 5,
+        in_specs=[vmem] * 3,
         out_specs=hbm,
         scratch_shapes=[pltpu.VMEM((LEAVES, PTS, NVEC), F32), dma((LEAVES,))],
         compiler_params=pltpu.CompilerParams(vmem_limit_bytes=24 * 2**20),

time: 42 us -> 37.2 us (0.89)
  Pallas kernels: 41.3 us -> 36.4 us
    pallas_call x1, Pallas kernels: 37.5 us -> 33.7 us  [shards(): pl.pallas_call(exchange, out_shape=[pltpu.VMEM((LEAVES, PTS, NVEC), F32),...]
    pallas_call x1, Pallas kernels: 3.79 us -> 2.73 us  [shards(): pl.pallas_call(finish, out_shape=shape((LEAVES, PTS, NVEC), F32), in_spec...]
where the time goes in v2:
time: 37.2 us; the launch traced here: 37.1 us
  Pallas kernels  36.4 us (98%)
  between operations  0.66 us (2%)
    pallas_call x1, Pallas kernels, shards(): pl.pallas_call(exchange, out_shape=[pltpu.VMEM((LEAVES, PTS, NVEC), F32),...  33.7 us
    pallas_call x1, Pallas kernels, shards(): pl.pallas_call(finish, out_shape=shape((LEAVES, PTS, NVEC), F32), in_spec...  2.73 us

profile of v2, /device:TPU:1, one launch (start us, length us, event | category | flops | bytes accessed | tf_op | source)
XLA Modules:
  0.0 37.1 jit_solution(16108972623904743855)
XLA Ops:
  0.7 33.7 %shard_map.127 = (f32[12,256,256]{2,1,0:T(8,128)S(1)}, bf16[12,256,256]{2,1,0:T(8,128)(2,1)S(1)}, bf16[384,256]{1,0:T(8,128)(2,1)S(1)}) custom-call(f32[12,256,256]{2,1,0:T(8,128)} %cot.1, f32[12,256,128]{2,1,0:T(8,128)} %rb.1, f32[12,256,128]{2,1,0:T(8,128)} %cb.1, f32[12,128,128]{2,1,0:T(8,128)} %lu.1, f32[1,128,128]{2,1,0:T(8,128)} %nu.1, ...), custom_call_target="tpu_custom_call" | custom-call | tf_op jit(solution)/shard_map/pallas_call | solution.py:374
  34.3 2.7 %shard_map.128 = f32[12,256,256]{2,1,0:T(8,128)} custom-call(f32[12,256,256]{2,1,0:T(8,128)S(1)} %get-tuple-element.8.near, bf16[12,256,256]{2,1,0:T(8,128)(2,1)S(1)} %get-tuple-element.9.mm, bf16[384,256]{1,0:T(8,128)(2,1)S(1)} %get-tuple-element.10.nt), custom_call_target="tpu_custom_call" | custom-call | tf_op jit(solution)/shard_map/pallas_call | solution.py:427

commit v3 on v2

--- a/solution.py
+++ b/solution.py
@@ -11,8 +11,8 @@
 F32, BF16 = jnp.float32, jnp.bfloat16
 LEAVES, PTS, RANK, NVEC = 12, 256, 128, 256
 REACH, NNEAR = 2, 4
-PIECES = 4
-CHUNK = 3
+PIECES = 1
+CHUNK = 6
 CHUNKS = LEAVES // CHUNK
 AHEAD = 3
 PIECE = PTS // PIECES
@@ -39,7 +39,7 @@
     cot, rb, cb, lu, nu, nc, gc, nd, ld, nb, ni_hbm, fn_hbm, fg,
     near_out, mm_out, nt_out,
     cotv, rbv, cbv, luv, nuv, ncv, gcv, ndv, ldv, nbv,
-    cth, ctl, up_sum, upv, sib, abuf, bbuf, cbuf, outv, ni, fn,
+    cth, ctl, up_sum, upv, sib, abuf, bbuf, cbuf, outv, gch, gcl, ni, fn,
     leaf_sem, small_sem, cb_sem, nb_sem,
     sa, ra, sb, rb_, sc, rc, ss, rs, sg, rg, sh, rh, int_sem,
 ):
@@ -220,6 +220,8 @@
     for c in groups:
         c.start()
 
+    send_halo(0, 2)
+
     @pl.loop(0, LEAVES, unroll=2)
     def _(leaf):
         prepare(REACH + leaf)
@@ -262,24 +264,24 @@
         second[-1].start()
 
     relays = []
+
+    def pass_on(*steps):
+        for step in steps:
+            arrived(sib, ss, rs, step).wait_recv()
+            relays.append(relay(sib, ss, rs, step))
+            relays[-1].start()
+
     for step in range(1, SIDE):
         arrived(gcv, sg, rg, step).wait_recv()
         relays.append(relay(gcv, sg, rg, step))
         relays[-1].start()
 
-    send_halo(0, 8)
-
     for c in siblings:
         c.start()
 
     @pl.loop(2, 8)
     def _(leaf):
         near(leaf)
-
-    for step in range(1, SIDE):
-        arrived(sib, ss, rs, step).wait_recv()
-        relays.append(relay(sib, ss, rs, step))
-        relays[-1].start()
 
     def from_twin(buf, send, recv, step):
         at = 0 if step == 0 else SIDE - 1 + step
@@ -290,19 +292,28 @@
 
     for step in range(SIDE):
         from_twin(gcv, sg, rg, step).wait_recv()
+
+    @pl.loop(0, NARROW)
+    def _(j):
+        rows = pl.ds(pl.multiple_of(j * RANK, RANK), RANK)
+        gch[rows, :], gcl[rows, :] = split(gcv[j, :RANK, :])
+
     for i, (dz, dx) in enumerate(OFFSETS):
         source = far(dz, dx, -1)[0]
         pltpu.make_async_remote_copy(
             bbuf.at[source], bbuf.at[source], sb.at[i], rb_.at[i], device_id=far(dz, dx, 1), device_id_type=MESH
         ).wait_recv()
 
-    part = jnp.zeros((SLICE, RANK), F32)
+    picked = []
     for j in range(NARROW):
         tag = jnp.concatenate([gcv[j, RANK:, :]] * (SLICE // 8), axis=0)
-        picked = bbuf[0]
+        value = bbuf[0]
         for g in range(1, WIDE):
-            picked = jnp.where(tag == float(g), bbuf[g], picked)
-        part += dot3(split(picked), split(gcv[j, :RANK, :]))
+            value = jnp.where(tag == float(g), bbuf[g], value)
+        picked.append(value)
+    high, low = split(jnp.concatenate(picked, axis=1))
+    both = dot(jnp.concatenate([high, low], axis=0), gch[...])
+    part = both[:SLICE] + both[SLICE:] + dot(high, gcl[...])
     mine = pl.ds(pl.multiple_of(n * SLICE, SLICE), SLICE)
     cbuf[mine, :] = part
     third = []
@@ -314,24 +325,26 @@
         )
         third[-1].start()
 
+    @pl.loop(0, REACH * PIECES)
+    def _(i):
+        for c in halo(i):
+            c.wait_recv()
+
+    for slot in (0, 1, REACH + LEAVES, REACH + LEAVES + 1):
+        prepare(slot)
+
+    @pl.loop(LEAVES - 2 * REACH, LEAVES)
+    def _(i):
+        near(i)
+
+    pass_on(1, 2, 3)
+
     for step in range(SIDE):
         from_twin(sib, ss, rs, step).wait_recv()
     node = jnp.zeros((NVEC, RANK), F32)
     for j in range(2):
         node += dot3(split(sib[jnp.clip(fn[0, j], 0, NARROW - 1)]), split(ncv[j]))
     outv[...] = node
-
-    @pl.loop(0, REACH * PIECES)
-    def _(i):
-        for c in halo(i):
-            c.wait_recv()
-
-    for slot in (0, 1, REACH + LEAVES, REACH + LEAVES + 1):
-        prepare(slot)
-
-    @pl.loop(LEAVES - 2 * REACH, LEAVES)
-    def _(i):
-        near(i)
 
     for d in range(1, NARROW):
         source = pl.ds(pl.multiple_of(lax.rem(n + NARROW - d, NARROW) * SLICE, SLICE), SLICE)
@@ -355,7 +368,7 @@
     def done(leaf):
         return pltpu.make_async_copy(buf.at[leaf], out.at[leaf], sem.at[leaf])
 
-    @pl.loop(0, LEAVES, unroll=2)
+    @pl.loop(0, LEAVES, unroll=6)
     def _(leaf):
         far = dot(mm[leaf], nt[: 2 * RANK]) + dot(mm[leaf, :, :RANK], nt[2 * RANK :])
         buf[leaf] = near[leaf] + far
@@ -400,6 +413,8 @@
             pltpu.VMEM((WIDE, SLICE, RANK), F32),
             pltpu.VMEM((NVEC, RANK), F32),
             pltpu.VMEM((NVEC, RANK), F32),
+            pltpu.VMEM((NARROW * RANK, RANK), BF16),
+            pltpu.VMEM((NARROW * RANK, RANK), BF16),
             pltpu.SMEM((NNEAR, LEAVES), jnp.int32),
             pltpu.SMEM((1, 2), jnp.int32),
             dma((3, CHUNKS)),

time: 37.2 us -> 35.6 us (0.957)
  Pallas kernels: 36.4 us -> 34.8 us
    pallas_call x1, Pallas kernels: 33.7 us -> 32.7 us  [shards(): pl.pallas_call(exchange, out_shape=[pltpu.VMEM((LEAVES, PTS, NVEC), F32),...]
    pallas_call x1, Pallas kernels: 2.73 us -> 2.15 us  [shards(): pl.pallas_call(finish, out_shape=shape((LEAVES, PTS, NVEC), F32), in_spec...]
where the time goes in v3:
time: 35.6 us; the launch traced here: 35.5 us
  Pallas kernels  34.8 us (98%)
  between operations  0.66 us (2%)
    pallas_call x1, Pallas kernels, shards(): pl.pallas_call(exchange, out_shape=[pltpu.VMEM((LEAVES, PTS, NVEC), F32),...  32.7 us
    pallas_call x1, Pallas kernels, shards(): pl.pallas_call(finish, out_shape=shape((LEAVES, PTS, NVEC), F32), in_spec...  2.15 us

profile of v3, /device:TPU:1, one launch (start us, length us, event | category | flops | bytes accessed | tf_op | source)
XLA Modules:
  0.0 35.5 jit_solution(17177602628041982430)
XLA Ops:
  0.7 32.7 %shard_map.127 = (f32[12,256,256]{2,1,0:T(8,128)S(1)}, bf16[12,256,256]{2,1,0:T(8,128)(2,1)S(1)}, bf16[384,256]{1,0:T(8,128)(2,1)S(1)}) custom-call(f32[12,256,256]{2,1,0:T(8,128)} %cot.1, f32[12,256,128]{2,1,0:T(8,128)} %rb.1, f32[12,256,128]{2,1,0:T(8,128)} %cb.1, f32[12,128,128]{2,1,0:T(8,128)} %lu.1, f32[1,128,128]{2,1,0:T(8,128)} %nu.1, ...), custom_call_target="tpu_custom_call" | custom-call | tf_op jit(solution)/shard_map/pallas_call | solution.py:387
  33.3 2.1 %shard_map.128 = f32[12,256,256]{2,1,0:T(8,128)} custom-call(f32[12,256,256]{2,1,0:T(8,128)S(1)} %get-tuple-element.8.near, bf16[12,256,256]{2,1,0:T(8,128)(2,1)S(1)} %get-tuple-element.9.mm, bf16[384,256]{1,0:T(8,128)(2,1)S(1)} %get-tuple-element.10.nt), custom_call_target="tpu_custom_call" | custom-call | tf_op jit(solution)/shard_map/pallas_call | solution.py:442

commit v4 on v3

--- a/solution.py
+++ b/solution.py
@@ -217,10 +217,10 @@
             both = dot(jnp.concatenate(split(cbv[leaf]), axis=1), jnp.concatenate([row, row], axis=0))
             mm_out[leaf] = jnp.concatenate(split(both[:, :RANK] + both[:, RANK:]), axis=1)
 
+    send_halo(0, 2)
+
     for c in groups:
         c.start()
-
-    send_halo(0, 2)
 
     @pl.loop(0, LEAVES, unroll=2)
     def _(leaf):
@@ -368,7 +368,7 @@
     def done(leaf):
         return pltpu.make_async_copy(buf.at[leaf], out.at[leaf], sem.at[leaf])
 
-    @pl.loop(0, LEAVES, unroll=6)
+    @pl.loop(0, LEAVES, unroll=12)
     def _(leaf):
         far = dot(mm[leaf], nt[: 2 * RANK]) + dot(mm[leaf, :, :RANK], nt[2 * RANK :])
         buf[leaf] = near[leaf] + far

time: 35.6 us -> 35.3 us (level)
  no operation moved by 1% of the time
where the time goes in v4:
time: 35.3 us; the launch traced here: 35.2 us
  Pallas kernels  34.5 us (98%)
  between operations  0.66 us (2%)
    pallas_call x1, Pallas kernels, shards(): pl.pallas_call(exchange, out_shape=[pltpu.VMEM((LEAVES, PTS, NVEC), F32),...  32.5 us
    pallas_call x1, Pallas kernels, shards(): pl.pallas_call(finish, out_shape=shape((LEAVES, PTS, NVEC), F32), in_spec...  2.05 us

profile of v4, /device:TPU:1, one launch (start us, length us, event | category | flops | bytes accessed | tf_op | source)
XLA Modules:
  0.0 35.2 jit_solution(8232146476482317075)
XLA Ops:
  0.7 32.5 %shard_map.127 = (f32[12,256,256]{2,1,0:T(8,128)S(1)}, bf16[12,256,256]{2,1,0:T(8,128)(2,1)S(1)}, bf16[384,256]{1,0:T(8,128)(2,1)S(1)}) custom-call(f32[12,256,256]{2,1,0:T(8,128)} %cot.1, f32[12,256,128]{2,1,0:T(8,128)} %rb.1, f32[12,256,128]{2,1,0:T(8,128)} %cb.1, f32[12,128,128]{2,1,0:T(8,128)} %lu.1, f32[1,128,128]{2,1,0:T(8,128)} %nu.1, ...), custom_call_target="tpu_custom_call" | custom-call | tf_op jit(solution)/shard_map/pallas_call | solution.py:387
  33.1 2.1 %shard_map.128 = f32[12,256,256]{2,1,0:T(8,128)} custom-call(f32[12,256,256]{2,1,0:T(8,128)S(1)} %get-tuple-element.8.near, bf16[12,256,256]{2,1,0:T(8,128)(2,1)S(1)} %get-tuple-element.9.mm, bf16[384,256]{1,0:T(8,128)(2,1)S(1)} %get-tuple-element.10.nt), custom_call_target="tpu_custom_call" | custom-call | tf_op jit(solution)/shard_map/pallas_call | solution.py:442

commit v5 on v4

--- a/solution.py
+++ b/solution.py
@@ -346,12 +346,13 @@
         node += dot3(split(sib[jnp.clip(fn[0, j], 0, NARROW - 1)]), split(ncv[j]))
     outv[...] = node
 
+    down = split(ndv[...])
     for d in range(1, NARROW):
         source = pl.ds(pl.multiple_of(lax.rem(n + NARROW - d, NARROW) * SLICE, SLICE), SLICE)
         pltpu.make_async_remote_copy(
             cbuf.at[source], cbuf.at[source], sc.at[d - 1], rc.at[d - 1], device_id=mate(d), device_id_type=MESH
         ).wait_recv()
-    node = outv[...] + dot3(split(cbuf[...]), split(ndv[...]), ((1,), (1,)))
+    node = outv[...] + dot3(split(cbuf[...]), down, ((1,), (1,)))
     high, low = split(node.T)
     nt_out[0:RANK], nt_out[RANK : 2 * RANK], nt_out[2 * RANK :] = high, high, low
 

time: 35.3 us -> 35.3 us (level)
  no operation moved by 1% of the time
where the time goes in v5:
time: 35.3 us; the launch traced here: 35.2 us
  Pallas kernels  34.5 us (98%)
  between operations  0.66 us (2%)
    pallas_call x1, Pallas kernels, shards(): pl.pallas_call(exchange, out_shape=[pltpu.VMEM((LEAVES, PTS, NVEC), F32),...  32.5 us
    pallas_call x1, Pallas kernels, shards(): pl.pallas_call(finish, out_shape=shape((LEAVES, PTS, NVEC), F32), in_spec...  2.05 us

profile of v5, /device:TPU:1, one launch (start us, length us, event | category | flops | bytes accessed | tf_op | source)
XLA Modules:
  0.0 35.2 jit_solution(17198504765922402790)
XLA Ops:
  0.7 32.5 %shard_map.127 = (f32[12,256,256]{2,1,0:T(8,128)S(1)}, bf16[12,256,256]{2,1,0:T(8,128)(2,1)S(1)}, bf16[384,256]{1,0:T(8,128)(2,1)S(1)}) custom-call(f32[12,256,256]{2,1,0:T(8,128)} %cot.1, f32[12,256,128]{2,1,0:T(8,128)} %rb.1, f32[12,256,128]{2,1,0:T(8,128)} %cb.1, f32[12,128,128]{2,1,0:T(8,128)} %lu.1, f32[1,128,128]{2,1,0:T(8,128)} %nu.1, ...), custom_call_target="tpu_custom_call" | custom-call | tf_op jit(solution)/shard_map/pallas_call | solution.py:388
  33.1 2.1 %shard_map.128 = f32[12,256,256]{2,1,0:T(8,128)} custom-call(f32[12,256,256]{2,1,0:T(8,128)S(1)} %get-tuple-element.8.near, bf16[12,256,256]{2,1,0:T(8,128)(2,1)S(1)} %get-tuple-element.9.mm, bf16[384,256]{1,0:T(8,128)(2,1)S(1)} %get-tuple-element.10.nt), custom_call_target="tpu_custom_call" | custom-call | tf_op jit(solution)/shard_map/pallas_call | solution.py:443
